TPU v7x, 32 devices: a whole 2x2x4 slice. The times are simulated.
32 devices in a mesh: groups: 2 (over y), wide: 8 (over z, core), narrow: 2 (over x).
Axes of the slice: x: 2, y: 2, z: 4, core: 2. Of those that a mesh axis runs over, the one named last changes fastest.
Arguments:
- blocks: bfloat16 [64, 128, 128, 128], P(('groups', 'wide'), None, 'narrow'), parts along dimension 0, may hold values from -6 to 6
- occupied: bfloat16 [16, 512, 512], P('groups', ('wide', 'narrow')), parts along dimension 0, may hold values from -0.5 to 0.5
- virtual: bfloat16 [16, 512, 512], P('groups', ('wide', 'narrow')), parts along dimension 0, may hold values from -0.5 to 0.5
- item_mu: int32 [64], P(('groups', 'wide')), parts along dimension 0, may hold values from 0 to 3
- item_nu: int32 [64], P(('groups', 'wide')), parts along dimension 0, may hold values from 0 to 3
- item_target: int32 [64], P(('groups', 'wide')), parts along dimension 0, may hold values from 0 to 15
- live_counts: int32 [16], P(('groups', 'wide')), parts along dimension 0, may hold values from 1 to 4, 21 in all
- target_occ: int32 [32], P('groups'), parts along dimension 0, may hold values from 0 to 3
- target_virt: int32 [32], P('groups'), parts along dimension 0, may hold values from 0 to 3
Outputs:
- transformed: bfloat16 [16, 16, 128, 128, 128], P('groups', None, 'wide', 'narrow'), parts along dimension 0
There are 2 independent parts, one for each index of `groups`. A program takes and returns all parts, laid end to end along the dimension named above; each array names one. Nothing has to cross between parts.
Inputs may be any that keep to these rules, and one draw needn't show every extreme that they name: The first live_counts[w] of the 4 slots of index w of wide are live; the counts sum to 21 and the largest is 4.
All inputs are finite; a program needn't handle non-finite values. No bound on the sum of `live_counts` on one device may be relied on, other than what follows from the above.
Results may differ from a plain program's by a relative error of at most 0.005.
Values may be sent and summed in bfloat16 or wider, within the bound.
A program may use at most 640 MiB of HBM per device.

v0:
```python
import math

import jax
import jax.numpy as jnp
from jax import lax
from jax.sharding import PartitionSpec as P


def lookup(indices, table):
    columns = jnp.arange(table.shape[0], dtype=jnp.int32)
    match = indices[:, None] == columns[None, :]
    return jnp.sum(jnp.where(match, table[None, :], 0), axis=1)


def contract_all(
    slabs, occ_five, virt_five, mu_all, nu_all, lam_all, sig_all, tgt_all, live, quarter, total
):
    items = slabs.shape[0]
    group = math.gcd(items, 16)

    def turn(counter, total):
        start = counter * group
        group_slabs = lax.dynamic_slice_in_dim(slabs, start, group, 0)
        group_mu = lax.dynamic_slice_in_dim(mu_all, start, group, 0)
        group_nu = lax.dynamic_slice_in_dim(nu_all, start, group, 0)
        group_lam = lax.dynamic_slice_in_dim(lam_all, start, group, 0)
        group_sig = lax.dynamic_slice_in_dim(sig_all, start, group, 0)
        group_tgt = lax.dynamic_slice_in_dim(tgt_all, start, group, 0)
        group_live = lax.dynamic_slice_in_dim(live, start, group, 0)
        virt_blocks = virt_five[:, group_nu, :, group_sig, :]
        occ_blocks = occ_five[:, group_lam, :, group_mu, :]
        sigma = total.shape[3]
        virt_blocks = lax.dynamic_slice_in_dim(virt_blocks, quarter * sigma, sigma, 3)
        half = jnp.einsum(
            "ipmn,itns->itpms", group_slabs, virt_blocks, preferred_element_type=jnp.float32
        ).astype(jnp.bfloat16)
        term = jnp.einsum("itpms,itlm->tipsl", half, occ_blocks, preferred_element_type=jnp.float32)
        term = term * group_live[None, :, None, None, None]
        return total.at[:, group_tgt].add(term)

    return lax.fori_loop(0, items // group, turn, total)


def local(
    blocks, occupied, virtual, item_mu, item_nu, item_target, live_counts, target_occ, target_virt
):
    slots = blocks.shape[0]
    width = blocks.shape[3]
    mu_all, nu_all, tgt_all, counts_all = (
        lax.all_gather(item_mu, "wide", axis=0, tiled=True),
        lax.all_gather(item_nu, "wide", axis=0, tiled=True),
        lax.all_gather(item_target, "wide", axis=0, tiled=True),
        lax.all_gather(live_counts, "wide", axis=0, tiled=True),
    )
    occ_full, virt_full = (
        lax.all_gather(occupied, ("wide", "narrow"), axis=1, tiled=True),
        lax.all_gather(virtual, ("wide", "narrow"), axis=1, tiled=True),
    )
    arrived = lax.all_to_all(blocks, "wide", split_axis=1, concat_axis=0, tiled=True)
    items = arrived.shape[0]
    order = jnp.arange(items, dtype=jnp.int32)
    owner = order // slots
    owner_count = lookup(owner, counts_all)
    live = (order % slots < owner_count).astype(jnp.float32)
    lam_all = lookup(tgt_all, target_occ)
    sig_all = lookup(tgt_all, target_virt)
    times = occ_full.shape[0]
    block_count = occ_full.shape[2] // width
    occ_five = occ_full.reshape(times, block_count, width, block_count, width)
    virt_five = virt_full.reshape(times, block_count, width, block_count, width)
    quarter = lax.axis_index("narrow")
    parts_narrow = lax.axis_size("narrow")
    targets = target_occ.shape[0]
    aux_rows = arrived.shape[1]
    gathered = lax.all_gather(arrived, "narrow", axis=2, tiled=True)
    sigma = width // parts_narrow
    start = jnp.zeros((times, targets, aux_rows, sigma, width), jnp.float32)
    total = contract_all(
        gathered,
        occ_five,
        virt_five,
        mu_all,
        nu_all,
        lam_all,
        sig_all,
        tgt_all,
        live,
        quarter,
        start,
    )
    return total.astype(jnp.bfloat16)


def solution(mesh):
    in_specs = (
        P(("groups", "wide"), None, "narrow", None),
        P("groups", ("wide", "narrow"), None),
        P("groups", ("wide", "narrow"), None),
        P(("groups", "wide")),
        P(("groups", "wide")),
        P(("groups", "wide")),
        P(("groups", "wide")),
        P("groups"),
        P("groups"),
    )
    out_specs = P("groups", None, "wide", "narrow", None)
    return jax.shard_map(local, mesh=mesh, in_specs=in_specs, out_specs=out_specs, check_vma=False)
```

profile of v0, /device:TPU:0, one launch (start us, length us, event | category | flops | bytes accessed | tf_op | source)
XLA Modules:
  0.0 897.2 jit_solution(15505893182382731963)
XLA Ops:
  7.3 9.8 %copy.31 = bf16[4,128,64,128]{3,2,0,1:T(8,128)(2,1)} copy(bf16[4,128,64,128]{3,2,1,0:T(8,128)(2,1)} %param.11) | data formatting | bytes 16777216 | tf_op args[0]
  17.1 6.3 all-to-all-start
  24.2 230.8 %all-to-all-done = bf16[4,128,64,128]{3,2,0,1:T(8,128)(2,1)} async-done(((bf16[4,128,64,128]{3,2,0,1:T(8,128)(2,1)}), bf16[4,128,64,128]{3,2,0,1:T(8,128)(2,1)}, u32[]{:S(2)}, u32[]{:S(2)}) %all-to-all-start) | async-done | bytes 8388640 | tf_op jit(solution)/shard_map/all_to_all | solution.py:59
  255.0 9.8 %copy.32 = bf16[8,4,16,64,128]{4,3,2,1,0:T(8,128)(2,1)} copy(bf16[8,4,16,64,128]{4,3,1,2,0:T(8,128)(2,1)} %bitcast.8) | data formatting | bytes 16777216 | tf_op jit(solution)/shard_map/all_to_all | solution.py:59
  268.4 6.8 all-reduce.4
  275.4 7.4 reshape.25
  282.8 5.8 copy.34
  288.5 7.1 reshape.24
  295.6 5.3 copy.33
  300.9 161.8 %all-gather.6.cloned.1.call-done = bf16[32,16,128,128]{3,2,1,0:T(8,128)(2,1)} async-done(((bf16[32,16,64,128]{3,2,1,0:T(8,128)(2,1)}), bf16[32,16,128,128]{3,2,1,0:T(8,128)(2,1)}) %all-gather.6.cloned.1.call-update) | async-done | bytes 16777232 | tf_op jit(solution)/shard_map/all_gather | solution.py:75
  462.7 21.2 %broadcast_in_dim.90 = f32[8,16,16,64,128]{4,3,2,1,0:T(8,128)} broadcast(f32[]{:T(128)} %constant.94.clone.1), dimensions={} | broadcast | bytes 67108864 | tf_op jit(solution)/shard_map/broadcast_in_dim | solution.py:77
  483.9 374.2 %while.15 = (s32[]{:T(128)}, f32[8,16,16,64,128]{4,3,2,1,0:T(8,128)}, s32[32]{0:T(128)S(1)}, s32[32]{0:T(128)S(1)}, s32[32]{0:T(128)S(1)}, /*index=5*/bf16[8,4,1...) while((s32[]{:T(128)}, ...), condition=%wide.region_5.6_spmd, body=%wide.region_3.5_spmd.sunk | while | flops 8640266240 | bytes 442500288 | solution.py:41
  489.4 5.3 gather_fusion
  494.7 5.4 constant_dynamic-slice_fusion.2
  503.8 28.8 %multiply_bitcast_fusion.2 = f32[16,8,16,64,128]{4,3,2,0,1:T(8,128)} fusion(f32[16]{0:T(128)S(1)} %dynamic_slice.94, bf16[32,16,128,128]{3,2,1,0:T(8,128)(2,1)} %get-tuple-element.468, s32[]{:T(128)S(6)} %select_n.145, bf16[16,8,128,64]{2,3,0,1:T(8,128)(2,1)S(1)} %copy.46, bf16[16,8,128,128]{3,2,1,0:T(8,128)(2,1)} %gather_fusion.1), kind=kOutput, calls=%fused_computation.3.clone.1 | convolution fusion | flops 8623489024 | bytes 81788992 | tf_op jit(solution)/shard_map/while/body/eval_jaxpr/itpms,itlm->tipsl/dot_general | solution.py:37
  532.6 43.6 %copy.47 = f32[16,8,16,64,128]{4,3,2,1,0:T(8,128)} copy(f32[16,8,16,64,128]{4,3,2,0,1:T(8,128)} %multiply_bitcast_fusion.2) | data formatting | bytes 134217728 | tf_op jit(solution)/shard_map/while/body/eval_jaxpr/mul | solution.py:38
  576.2 94.9 %scatter_fusion = f32[8,16,16,64,128]{4,3,2,1,0:T(8,128)} fusion(f32[8,16,16,64,128]{4,3,2,1,0:T(8,128)} %get-tuple-element.446, s32[16]{0:T(128)S(1)} %get-tuple-element.427, f32[16,8,16,64,128]{4,3,2,1,0:T(8,128)} %copy.47), kind=kCustom, calls=%fused_computation.2.clone.1 | custom fusion | flops 16777216 | bytes 201326656 | tf_op jit(solution)/shard_map/while/body/eval_jaxpr/scatter-add | solution.py:39
  671.3 5.2 gather_fusion.1
  676.5 5.3 gather_fusion
  681.8 5.4 constant_dynamic-slice_fusion.2
  690.9 28.8 %multiply_bitcast_fusion.2 = f32[16,8,16,64,128]{4,3,2,0,1:T(8,128)} fusion(f32[16]{0:T(128)S(1)} %dynamic_slice.94, bf16[32,16,128,128]{3,2,1,0:T(8,128)(2,1)} %get-tuple-element.468, s32[]{:T(128)S(6)} %select_n.145, bf16[16,8,128,64]{2,3,0,1:T(8,128)(2,1)S(1)} %copy.46, bf16[16,8,128,128]{3,2,1,0:T(8,128)(2,1)} %gather_fusion.1), kind=kOutput, calls=%fused_computation.3.clone.1 | convolution fusion | flops 8623489024 | bytes 81788992 | tf_op jit(solution)/shard_map/while/body/eval_jaxpr/itpms,itlm->tipsl/dot_general | solution.py:37
  719.7 43.6 %copy.47 = f32[16,8,16,64,128]{4,3,2,1,0:T(8,128)} copy(f32[16,8,16,64,128]{4,3,2,0,1:T(8,128)} %multiply_bitcast_fusion.2) | data formatting | bytes 134217728 | tf_op jit(solution)/shard_map/while/body/eval_jaxpr/mul | solution.py:38
  763.2 94.9 %scatter_fusion = f32[8,16,16,64,128]{4,3,2,1,0:T(8,128)} fusion(f32[8,16,16,64,128]{4,3,2,1,0:T(8,128)} %get-tuple-element.446, s32[16]{0:T(128)S(1)} %get-tuple-element.427, f32[16,8,16,64,128]{4,3,2,1,0:T(8,128)} %copy.47), kind=kCustom, calls=%fused_computation.2.clone.1 | custom fusion | flops 16777216 | bytes 201326656 | tf_op jit(solution)/shard_map/while/body/eval_jaxpr/scatter-add | solution.py:39
  858.1 32.6 %convert_element_type.19 = bf16[8,16,16,64,128]{4,3,2,1,0:T(8,128)(2,1)} convert(f32[8,16,16,64,128]{4,3,2,1,0:T(8,128)} %get-tuple-element.283) | non-fusion elementwise | flops 16777216 | bytes 100663296 | tf_op jit(solution)/shard_map/convert_element_type | solution.py:91
  (42 shorter events, 17.0 us)
Async XLA Ops:
  6.5 268.9 %all-gather.8.cloned.1.call-start = ((), (), s32[]{:S(2)}) async-start(), calls=%async_computation.3 | async-start | bytes 4456448 | tf_op jit(solution)/shard_map/all_gather | solution.py:56
  17.1 237.9 %all-to-all-start = ((bf16[4,128,64,128]{3,2,0,1:T(8,128)(2,1)}), bf16[4,128,64,128]{3,2,0,1:T(8,128)(2,1)}, u32[]{:S(2)}, u32[]{:S(2)}) async-start(bf16[4,128,64,128]{3,2,0,1:T(8,128)(2,1)} %copy.31), calls=%async_computation | async-start | bytes 16777216 | tf_op jit(solution)/shard_map/all_to_all | solution.py:59
  23.4 265.1 %all-gather.4.cloned.1.call-start = ((), (), s32[]{:S(2)}) async-start(), calls=%async_computation.1 | async-start | bytes 4456448 | tf_op jit(solution)/shard_map/all_gather | solution.py:57
  24.1 438.6 %all-gather.6.cloned.1.call-start = ((), (), s32[]{:S(2)}) async-start(), calls=%async_computation.2 | async-start | bytes 25165824 | tf_op jit(solution)/shard_map/all_gather | solution.py:75
  264.8 0.7 copy-start.5
  264.8 2.1 copy-start.2
  264.8 2.4 copy-start.3
  264.8 2.6 copy-start.4
  264.8 10.5 %copy-start = (s32[16]{0:T(128)S(1)}, s32[16]{0:T(128)}, u32[]{:S(2)}) copy-start(s32[16]{0:T(128)} %param.18) | copy-start | bytes 196
  264.8 10.5 %copy-start.1 = (s32[16]{0:T(128)S(1)}, s32[16]{0:T(128)}, u32[]{:S(2)}) copy-start(s32[16]{0:T(128)} %param.19) | copy-start | bytes 196
Sparse Core Ops, SparseCore 0:
  9.5 98.8 all-gather.7
  110.7 117.9 all-gather.3
  264.9 197.7 all-gather.5
where the time goes:
time: 898 us; the launch traced here: 897 us
  waiting for transfers between devices  394 us (44%)
  other arithmetic  223 us (25%)
  local copies, waits for them, and re-layouts  195 us (22%)
  matrix products  57.6 us (6%)
  between operations  14.6 us (2%)
    all_to_all x1, waiting for transfers between devices, local(): lax.all_to_all(blocks, 'wide', split_axis=1, concat_axis=0, tiled=True)  231 us
    scatter-add x2, other arithmetic, turn(): return total.at[:, group_tgt].add(term)  190 us
    all_gather x1, waiting for transfers between devices, local(): gathered = lax.all_gather(arrived, 'narrow', axis=2, tiled=True)  162 us
    mul x2, local copies, waits for them, and re-layouts, turn(): term = term * group_live[None, :, None, None, None]  87.1 us
    dot_general x2, matrix products, turn(): jnp.einsum('itpms,itlm->tipsl', half, occ_blocks, preferred_element_type=...  57.6 us
    convert_element_type x1, other arithmetic, local(): return total.astype(jnp.bfloat16)  32.6 us
    broadcast_in_dim x1, local copies, waits for them, and re-layouts, local(): start = jnp.zeros((times, targets, aux_rows, sigma, width), jnp.float32)  21.2 us
  transfers between devices with their start and end apart: 4, of which 2 were waited for; matrix products, arithmetic and copies ran while one was open for 5% of the time, Pallas kernels for 0%

commit v1 on v0

v1 whole, which is shorter than its diff:
```python
import functools

import jax
import jax.numpy as jnp
from jax import lax
from jax.experimental import pallas as pl
from jax.experimental.pallas import tpu as pltpu
from jax.sharding import PartitionSpec as P

MESH = pl.DeviceIdType.MESH
NT_DIMS = (((1,), (1,)), ((), ()))


def offset_of(turn, wide):
    sign = 1 - 2 * lax.rem(turn, 2)
    return wide // 2 + sign * lax.div(turn + 1, 2)


def exchange_kernel(
    wide, narrow, lag, blocks, gathered, own_sem, z_send, z_recv, x_send, x_recv, xo_send, xo_recv
):
    slots = blocks.shape[0]
    rows = gathered.shape[1]
    mrows = blocks.shape[2]
    me = lax.axis_index("wide")
    here = lax.axis_index("narrow")
    sends = slots * (wide - 1)

    barrier = pltpu.get_barrier_semaphore()

    def greet(step, carry):
        peer = lax.rem(me + step, wide)
        pl.semaphore_signal(barrier, inc=1, device_id={"wide": peer}, device_id_type=MESH)
        return carry

    lax.fori_loop(1, wide, greet, 0)
    for step in range(1, narrow):
        peer = lax.rem(here + step, narrow)
        pl.semaphore_signal(barrier, inc=1, device_id={"narrow": peer}, device_id_type=MESH)
    pl.semaphore_wait(barrier, wide - 1 + narrow - 1)

    columns = pl.ds(pl.multiple_of(here * mrows, mrows), mrows)

    def place(slot):
        return gathered.at[slot, :, columns, :]

    def rows_for(slot, device):
        return blocks.at[slot, pl.ds(device * rows, rows)]

    def z_copy(turn):
        slot = lax.div(turn, wide - 1)
        peer = lax.rem(me + offset_of(lax.rem(turn, wide - 1), wide), wide)
        return pltpu.make_async_remote_copy(
            src_ref=rows_for(slot, peer),
            dst_ref=place(me * slots + slot),
            send_sem=z_send.at[turn],
            recv_sem=z_recv.at[turn],
            device_id={"wide": peer},
            device_id_type=MESH,
        )

    def x_copy(turn, step):
        slot = lax.div(turn, wide - 1)
        offset = offset_of(lax.rem(turn, wide - 1), wide)
        source = lax.rem(me + wide - offset, wide)
        return pltpu.make_async_remote_copy(
            src_ref=place(source * slots + slot),
            dst_ref=place(source * slots + slot),
            send_sem=x_send.at[step - 1, turn],
            recv_sem=x_recv.at[step - 1, turn],
            device_id={"narrow": lax.rem(here + step, narrow)},
            device_id_type=MESH,
        )

    def own_x_copy(slot, step):
        return pltpu.make_async_remote_copy(
            src_ref=rows_for(slot, me),
            dst_ref=place(me * slots + slot),
            send_sem=xo_send.at[step - 1, slot],
            recv_sem=xo_recv.at[step - 1, slot],
            device_id={"narrow": lax.rem(here + step, narrow)},
            device_id_type=MESH,
        )

    def own_copy(slot):
        return pltpu.make_async_copy(
            rows_for(slot, me), place(me * slots + slot), own_sem.at[slot]
        )

    def begin(turn, carry):
        z_copy(turn).start()
        return carry

    def forward(turn, carry):
        z_copy(turn).wait_recv()
        for step in range(1, narrow):
            x_copy(turn, step).start()
        return carry

    def both(turn, carry):
        begin(turn, carry)
        return forward(turn - lag, carry)

    lax.fori_loop(0, lag, begin, 0)
    for slot in range(slots):
        for step in range(1, narrow):
            own_x_copy(slot, step).start()
        own_copy(slot).start()
    lax.fori_loop(lag, sends, both, 0)
    lax.fori_loop(sends - lag, sends, forward, 0)

    def finish(turn, carry):
        z_copy(turn).wait_send()
        for step in range(1, narrow):
            x_copy(turn, step).wait()
        return carry

    for slot in range(slots):
        own_copy(slot).wait()
        for step in range(1, narrow):
            own_x_copy(slot, step).wait()
    lax.fori_loop(0, sends, finish, 0)


def exchange(blocks):
    slots, aux, mrows, width = blocks.shape
    wide = lax.axis_size("wide")
    narrow = lax.axis_size("narrow")
    sends = slots * (wide - 1)
    return pl.pallas_call(
        functools.partial(exchange_kernel, wide, narrow, min(4, sends)),
        out_shape=jax.ShapeDtypeStruct(
            (wide * slots, aux // wide, narrow * mrows, width), blocks.dtype
        ),
        in_specs=[pl.BlockSpec(memory_space=pl.ANY)],
        out_specs=pl.BlockSpec(memory_space=pl.ANY),
        scratch_shapes=[
            pltpu.SemaphoreType.DMA((slots,)),
            pltpu.SemaphoreType.DMA((sends,)),
            pltpu.SemaphoreType.DMA((sends,)),
            pltpu.SemaphoreType.DMA((narrow - 1, sends)),
            pltpu.SemaphoreType.DMA((narrow - 1, sends)),
            pltpu.SemaphoreType.DMA((narrow - 1, slots)),
            pltpu.SemaphoreType.DMA((narrow - 1, slots)),
        ],
        compiler_params=pltpu.CompilerParams(collective_id=0, has_side_effects=True),
        name="exchange",
    )(blocks)


def contract_kernel(meta, x_ref, virt_ref, occ_ref, out_ref, total, half):
    turn = pl.program_id(0)
    times, rows, sigma, width = total.shape
    kind = meta[2, turn]
    occ_row = pl.multiple_of(meta[3, turn] * width, width)
    occ_column = pl.multiple_of(meta[4, turn] * width, width)
    virt_row = pl.multiple_of(meta[5, turn] * sigma, sigma)
    virt_column = pl.multiple_of(meta[6, turn] * width, width)

    @pl.when(kind == 4)
    def _():
        out_ref[...] = jnp.zeros_like(out_ref)

    @pl.when(kind < 4)
    def _():
        virt = jnp.concatenate(
            [
                virt_ref[time, pl.ds(virt_row, sigma), pl.ds(virt_column, width)]
                for time in range(times)
            ],
            axis=0,
        )
        for row in range(0, rows, 2):
            pair = x_ref[0, row : row + 2].reshape(2 * width, width)
            product = lax.dot_general(
                virt, pair, NT_DIMS, preferred_element_type=jnp.float32
            ).astype(jnp.bfloat16)
            half[:, row] = product[:, :width].reshape(times, sigma, width)
            half[:, row + 1] = product[:, width:].reshape(times, sigma, width)

    def second(first, last):
        def step(time, carry):
            occ = occ_ref[time, pl.ds(occ_row, width), pl.ds(occ_column, width)]
            term = lax.dot_general(
                half[time].reshape(rows * sigma, width),
                occ,
                NT_DIMS,
                preferred_element_type=jnp.float32,
            ).reshape(rows, sigma, width)
            if not first:
                term = term + total[time]
            if last:
                out_ref[time, 0] = term.astype(out_ref.dtype)
            else:
                total[time] = term
            return carry

        lax.fori_loop(0, times, step, 0, unroll=2)

    for code in range(4):

        @pl.when(kind == code)
        def _(code=code):
            second(code % 2 == 1, code // 2 == 1)


def contract(meta, gathered, virt, occ, targets):
    items, rows, width, _ = gathered.shape
    times = occ.shape[0]
    sigma = virt.shape[1] // (virt.shape[2] // width)
    per_item = 4 * times * rows * sigma * width * width
    grid_spec = pltpu.PrefetchScalarGridSpec(
        num_scalar_prefetch=1,
        grid=(meta.shape[1],),
        in_specs=[
            pl.BlockSpec((1, rows, width, width), lambda j, meta: (meta[0, j], 0, 0, 0)),
            pl.BlockSpec(virt.shape, lambda j, meta: (0, 0, 0)),
            pl.BlockSpec(occ.shape, lambda j, meta: (0, 0, 0)),
        ],
        out_specs=pl.BlockSpec(
            (times, 1, rows, sigma, width), lambda j, meta: (0, meta[1, j], 0, 0, 0)
        ),
        scratch_shapes=[
            pltpu.VMEM((times, rows, sigma, width), jnp.float32),
            pltpu.VMEM((times, rows, sigma, width), jnp.bfloat16),
        ],
    )
    return pl.pallas_call(
        contract_kernel,
        grid_spec=grid_spec,
        out_shape=jax.ShapeDtypeStruct((times, targets, rows, sigma, width), jnp.bfloat16),
        compiler_params=pltpu.CompilerParams(
            dimension_semantics=("arbitrary",), vmem_limit_bytes=48 * 1024 * 1024
        ),
        cost_estimate=pl.CostEstimate(
            flops=per_item * items,
            bytes_accessed=2 * times * targets * rows * sigma * width + 2 * gathered.size,
            transcendentals=0,
        ),
        name="contract",
    )(meta, gathered, virt, occ)


def work_list(lists, slots, target_occ, target_virt):
    mu, nu, target = (lists[:, k * slots : (k + 1) * slots].reshape(-1) for k in range(3))
    items = target.shape[0]
    targets = target_occ.shape[0]
    live = (jnp.arange(slots)[None, :] < lists[:, 3 * slots :]).reshape(-1)
    names = jnp.arange(targets, dtype=jnp.int32)
    named = jnp.any((target[None, :] == names[:, None]) & live[None, :], axis=1)
    valid = jnp.concatenate([live, ~named])
    key = jnp.concatenate([target, names])
    order = jnp.arange(items + targets, dtype=jnp.int32)
    same = valid[None, :] & (key[None, :] == key[:, None])
    ahead = order[None, :] < order[:, None]
    first = ~jnp.any(same & ahead, axis=1)
    last = ~jnp.any(same & (order[None, :] > order[:, None]), axis=1)
    before = valid[None, :] & ((key[None, :] < key[:, None]) | (same & ahead))
    rank = jnp.sum(before, axis=1, dtype=jnp.int32)
    blank = jnp.zeros((targets,), jnp.int32)
    is_item = order < items
    kind = jnp.where(is_item, first.astype(jnp.int32) + 2 * last.astype(jnp.int32), 4)
    at_target = key[:, None] == names[None, :]
    lam = jnp.sum(jnp.where(at_target, target_occ[None, :], 0), axis=1)
    sig = jnp.sum(jnp.where(at_target, target_virt[None, :], 0), axis=1)
    table = jnp.stack(
        [
            jnp.where(is_item, order, 0),
            key,
            kind,
            lam,
            jnp.concatenate([mu, blank]),
            sig,
            jnp.concatenate([nu, blank]),
        ]
    )
    steps = jnp.sum(valid, dtype=jnp.int32)
    chosen = valid[None, :] & (rank[None, :] == jnp.minimum(order, steps - 1)[:, None])
    meta = jnp.sum(jnp.where(chosen[None], table[:, None, :], 0), axis=2, dtype=jnp.int32)
    return meta.at[2].set(jnp.where(order < steps, meta[2], 5))


def local(
    blocks, occupied, virtual, item_mu, item_nu, item_target, live_counts, target_occ, target_virt
):
    slots = blocks.shape[0]
    width = blocks.shape[3]
    narrow = lax.axis_size("narrow")
    sigma = width // narrow
    own = jnp.concatenate([item_mu, item_nu, item_target, live_counts])
    lists = lax.all_gather(own, "wide", axis=0, tiled=False)
    times, _, across = virtual.shape
    virt = virtual.reshape(times, -1, across // width, narrow, sigma)
    virt = lax.all_to_all(virt, "narrow", split_axis=3, concat_axis=1, tiled=True)
    virt = virt.reshape(times, -1, across // narrow)
    virt = lax.all_gather(virt, "wide", axis=1, tiled=True)
    occ = lax.all_gather(occupied, "wide", axis=1, tiled=False)
    occ = lax.all_gather(occ, "narrow", axis=2, tiled=False)
    occ = occ.reshape(times, -1, across)
    virt = virt.transpose(0, 2, 1)
    meta = work_list(lists, slots, target_occ, target_virt)
    gathered = exchange(blocks)
    return contract(meta, gathered, virt, occ, target_occ.shape[0])


def solution(mesh):
    in_specs = (
        P(("groups", "wide"), None, "narrow", None),
        P("groups", ("wide", "narrow"), None),
        P("groups", ("wide", "narrow"), None),
        P(("groups", "wide")),
        P(("groups", "wide")),
        P(("groups", "wide")),
        P(("groups", "wide")),
        P("groups"),
        P("groups"),
    )
    out_specs = P("groups", None, "wide", "narrow", None)
    return jax.shard_map(local, mesh=mesh, in_specs=in_specs, out_specs=out_specs, check_vma=False)
```

time: 898 us -> 367 us (0.41)
  waiting for transfers between devices: 394 us -> 21.3 us
  Pallas kernels: 0 us -> 301 us
  other arithmetic: 223 us -> 2.41 us
  local copies, waits for them, and re-layouts: 195 us -> 8.08 us
  matrix products: 57.6 us -> 0 us
  blocking collectives: 6.78 us -> 16.9 us
    pallas_call x0 -> x2, Pallas kernels: none -> 301 us  [the longest x1 250 us: exchange(): pl.pallas_call(functools.partial(exchange_kernel, wide, narrow, min(4, se...]
    all_to_all x1 -> x0, waiting for transfers between devices: 231 us -> none  [local(): lax.all_to_all(blocks, 'wide', split_axis=1, concat_axis=0, tiled=True)]
    scatter-add x2 -> x0, other arithmetic: 190 us -> none  [turn(): return total.at[:, group_tgt].add(term)]
    all_gather x3, waiting for transfers between devices: 162 us -> 20.5 us  [the longest x1 20.5 us: local(): occ = lax.all_gather(occupied, 'wide', axis=1, tiled=False)]
    mul x2 -> x0, local copies, waits for them, and re-layouts: 87.1 us -> none  [turn(): term = term * group_live[None, :, None, None, None]]
    dot_general x2 -> x0, matrix products: 57.6 us -> none  [turn(): jnp.einsum('itpms,itlm->tipsl', half, occ_blocks, preferred_element_type=...]
    convert_element_type x2 -> x0, other arithmetic: 32.6 us -> none  [the longest x1 32.6 us: local(): return total.astype(jnp.bfloat16)]
    broadcast_in_dim x1 -> x0, local copies, waits for them, and re-layouts: 21.2 us -> none  [local(): start = jnp.zeros((times, targets, aux_rows, sigma, width), jnp.float32)]
  transfers between devices with their start and end apart: 4 -> 3, of which waited for: 2 -> 1; matrix products, arithmetic and copies ran while one was open for 5% -> 3% of each run, Pallas kernels for 0% -> 68%
where the time goes in v1:
time: 367 us; the launch traced here: 365 us
  Pallas kernels  301 us (82%)
  waiting for transfers between devices  21.3 us (6%)
  blocking collectives  16.9 us (5%)
  between operations  15.3 us (4%)
  local copies, waits for them, and re-layouts  8.08 us (2%)
    pallas_call x1, Pallas kernels, exchange(): pl.pallas_call(functools.partial(exchange_kernel, wide, narrow, min(4, se...  250 us
    pallas_call x1, Pallas kernels, contract(): pl.pallas_call(contract_kernel, grid_spec=grid_spec, out_shape=jax.ShapeD...  51.4 us
    all_gather x1, waiting for transfers between devices, local(): occ = lax.all_gather(occupied, 'wide', axis=1, tiled=False)  20.5 us
    all_to_all x1, blocking collectives, local(): lax.all_to_all(virt, 'narrow', split_axis=3, concat_axis=1, tiled=True)  9.18 us
    unnamed x1, blocking collectives  7.77 us
  transfers between devices with their start and end apart: 3, of which 1 were waited for; matrix products, arithmetic and copies ran while one was open for 3% of the time, Pallas kernels for 68%

profile of v1, /device:TPU:0, one launch (start us, length us, event | category | flops | bytes accessed | tf_op | source)
XLA Modules:
  0.0 365.3 jit_solution(12158998107994137695)
XLA Ops:
  6.5 0.7 all-gather.9.cloned.1.call-update
  7.3 1.3 reshape.163
  8.6 0.2 copy.27
  8.8 0.4 reshape.177
  9.2 9.2 %all_to_all.15 = bf16[2,2,32768]{2,1,0:T(2,128)(2,1)S(1)} all-to-all(bf16[2,2,32768]{2,1,0:T(2,128)(2,1)S(1)} %reshape.177), channel_id=1, replica_groups=mesh['groups'=2,'wide'=8,'narrow'=2] {'narrow'}, dimensions={0} | all-to-all | bytes 524288 | tf_op jit(solution)/shard_map/all_to_all | solution.py:294
  18.4 0.3 reshape.178
  18.8 0.2 bitcast_bitcast_fusion
  19.0 0.2 copy.24
  19.2 1.0 reshape.175
  20.3 20.5 %all-gather.9.cloned.1.call-done = bf16[8,256,512]{2,1,0:T(8,128)(2,1)} async-done(((bf16[8,32,512]{2,1,0:T(8,128)(2,1)}), bf16[8,256,512]{2,1,0:T(8,128)(2,1)}) %all-gather.9.cloned.1.call-update) | async-done | bytes 2097168 | tf_op jit(solution)/shard_map/all_gather | solution.py:297
  41.5 0.7 dynamic-slice.8
  42.9 0.2 add_dynamic-update-slice_fusion
  43.1 7.8 %all-reduce.2 = s32[104]{0:T(128)S(1)} all-reduce(s32[104]{0:T(128)S(1)} %add_dynamic-update-slice_fusion), channel_id=2, replica_groups=mesh['groups'=2,'wide'=8,'narrow'=2] {'wide'}, use_global_device_ids=true, to_apply=%add.2 | all-reduce | flops 104 | bytes 832
  50.9 0.2 slice_reduce_fusion
  51.2 0.1 lt.87
  51.5 0.1 fusion.5
  51.7 249.7 %exchange.1.x_ref = bf16[32,16,128,128]{3,2,1,0:T(8,128)(2,1)} custom-call(bf16[4,128,64,128]{3,2,1,0:T(8,128)(2,1)} %blocks.1), custom_call_target="tpu_custom_call" | custom-call | tf_op jit(solution)/shard_map/exchange/pallas_call | solution.py:130
  301.4 0.7 convert_reduce_fusion.1
  302.8 0.2 convert_reduce_fusion
  303.1 0.2 fusion.3
  303.3 0.2 select_reduce_fusion
  303.5 0.6 compare_select_fusion.2
  304.3 3.0 copy.23
  307.3 51.4 %contract.1 = bf16[8,16,16,64,128]{4,3,2,1,0:T(8,128)(2,1)} custom-call(s32[7,48]{1,0:T(8,128)S(1)} %scatter.4.meta, bf16[32,16,128,128]{3,2,1,0:T(8,128)(2,1)} %exchange.1.x_ref, bf16[8,256,512]{2,1,0:T(8,128)(2,1)S(1)} %bitcast.26, bf16[8,512,512]{2,1,0:T(8,128)(2,1)} %bitcast.32), custom_call_target="tpu_custom_call" | custom-call | flops 17179869184 | bytes 50331648 | tf_op jit(solution)/shard_map/contract/pallas_call | solution.py:228
  (35 shorter events, 0.8 us)
Async XLA Ops:
  6.5 34.3 %all-gather.9.cloned.1.call-start = ((), (), s32[]{:S(2)}) async-start(), calls=%async_computation.2 | async-start | bytes 2359296 | tf_op jit(solution)/shard_map/all_gather | solution.py:297
  7.3 297.0 %all-gather.7.cloned.1.call-start = ((), (), s32[]{:S(2)}) async-start(), calls=%async_computation.1 | async-start | bytes 2359296 | tf_op jit(solution)/shard_map/all_gather | solution.py:296
  8.6 32.9 %copy-start.5 = (u32[32]{0:T(128)S(1)}, u32[32]{0:T(128)}, u32[]{:S(2)}) copy-start(u32[32]{0:T(128)} %constant.55) | copy-start | bytes 388
  8.6 34.3 %copy-start.2 = (s32[4]{0:T(128)S(1)}, s32[4]{0:T(128)}, u32[]{:S(2)}) copy-start(s32[4]{0:T(128)} %param.16) | copy-start | bytes 52
  8.6 34.3 %copy-start.3 = (s32[4]{0:T(128)S(1)}, s32[4]{0:T(128)}, u32[]{:S(2)}) copy-start(s32[4]{0:T(128)} %param.15) | copy-start | bytes 52
  8.6 34.3 %copy-start.4 = (s32[4]{0:T(128)S(1)}, s32[4]{0:T(128)}, u32[]{:S(2)}) copy-start(s32[4]{0:T(128)} %param.14) | copy-start | bytes 52
  20.2 287.0 %all-gather.11.cloned.1.call-start = ((), (), s32[]{:S(2)}) async-start(), calls=%async_computation.3 | async-start | bytes 6291456 | tf_op jit(solution)/shard_map/all_gather | solution.py:298
  51.7 251.3 %copy-start = (s32[16]{0:T(128)S(1)}, s32[16]{0:T(128)}, u32[]{:S(2)}) copy-start(s32[16]{0:T(128)} %param.19) | copy-start | bytes 196
  51.7 251.3 %copy-start.1 = (s32[16]{0:T(128)S(1)}, s32[16]{0:T(128)}, u32[]{:S(2)}) copy-start(s32[16]{0:T(128)} %param.18) | copy-start | bytes 196
Sparse Core Ops, SparseCore 0:
  9.0 31.7 all-gather.8
  42.4 55.7 all-gather.6
  99.7 100.0 all-gather.10

commit v2 on v1

--- a/solution.py
+++ b/solution.py
@@ -294,9 +294,7 @@
     virt = lax.all_to_all(virt, "narrow", split_axis=3, concat_axis=1, tiled=True)
     virt = virt.reshape(times, -1, across // narrow)
     virt = lax.all_gather(virt, "wide", axis=1, tiled=True)
-    occ = lax.all_gather(occupied, "wide", axis=1, tiled=False)
-    occ = lax.all_gather(occ, "narrow", axis=2, tiled=False)
-    occ = occ.reshape(times, -1, across)
+    occ = lax.all_gather(occupied, ("wide", "narrow"), axis=1, tiled=True)
     virt = virt.transpose(0, 2, 1)
     meta = work_list(lists, slots, target_occ, target_virt)
     gathered = exchange(blocks)

time: 367 us -> 347 us (0.946)
  waiting for transfers between devices: 21.3 us -> 0.75 us
  Pallas kernels: 301 us -> 297 us
    all_gather x2 -> x1, waiting for transfers between devices: 20.5 us -> 0.02 us  [local(): occ = lax.all_gather(occupied, ('wide', 'narrow'), axis=1, tiled=True)]
    pallas_call x1, Pallas kernels: 250 us -> 246 us  [exchange(): pl.pallas_call(functools.partial(exchange_kernel, wide, narrow, min(4, se...]
  transfers between devices with their start and end apart: 3 -> 2, of which waited for: 1 -> 0; matrix products, arithmetic and copies ran while one was open for 3% -> 2% of each run, Pallas kernels for 68% -> 72%
where the time goes in v2:
time: 347 us; the launch traced here: 343 us
  Pallas kernels  297 us (86%)
  blocking collectives  18.6 us (5%)
  between operations  15.6 us (4%)
  local copies, waits for them, and re-layouts  8.71 us (3%)
    pallas_call x1, Pallas kernels, exchange(): pl.pallas_call(functools.partial(exchange_kernel, wide, narrow, min(4, se...  246 us
    pallas_call x1, Pallas kernels, contract(): pl.pallas_call(contract_kernel, grid_spec=grid_spec, out_shape=jax.ShapeD...  50.8 us
    unnamed x1, blocking collectives  9.39 us
    all_to_all x1, blocking collectives, local(): lax.all_to_all(virt, 'narrow', split_axis=3, concat_axis=1, tiled=True)  9.18 us
  transfers between devices with their start and end apart: 2, of which 0 were waited for; matrix products, arithmetic and copies ran while one was open for 2% of the time, Pallas kernels for 72%

profile of v2, /device:TPU:0, one launch (start us, length us, event | category | flops | bytes accessed | tf_op | source)
XLA Modules:
  0.0 343.3 jit_solution(5622513585880665054)
XLA Ops:
  6.5 1.3 reshape.160
  7.8 0.2 copy.27
  8.0 0.4 reshape.170
  8.4 9.2 %all_to_all.15 = bf16[2,2,32768]{2,1,0:T(2,128)(2,1)S(1)} all-to-all(bf16[2,2,32768]{2,1,0:T(2,128)(2,1)S(1)} %reshape.170), channel_id=1, replica_groups=mesh['groups'=2,'wide'=8,'narrow'=2] {'narrow'}, dimensions={0} | all-to-all | bytes 524288 | tf_op jit(solution)/shard_map/all_to_all | solution.py:294
  17.6 0.3 reshape.171
  18.0 0.2 bitcast_bitcast_fusion
  18.2 0.2 copy.24
  18.4 1.0 reshape.168
  19.5 0.7 all-gather.6.cloned.1.call-update
  20.8 1.3 dynamic-slice.8
  22.9 0.9 add_dynamic-update-slice_fusion
  23.7 9.4 %all-reduce.2 = s32[104]{0:T(128)S(1)} all-reduce(s32[104]{0:T(128)S(1)} %add_dynamic-update-slice_fusion), channel_id=2, replica_groups=mesh['groups'=2,'wide'=8,'narrow'=2] {'wide'}, use_global_device_ids=true, to_apply=%add.2 | all-reduce | flops 104 | bytes 832
  33.2 0.2 slice_reduce_fusion
  33.5 0.1 lt.87
  33.8 0.1 fusion.5
  34.0 245.7 %exchange.1.x_ref = bf16[32,16,128,128]{3,2,1,0:T(8,128)(2,1)} custom-call(bf16[4,128,64,128]{3,2,1,0:T(8,128)(2,1)} %blocks.1), custom_call_target="tpu_custom_call" | custom-call | tf_op jit(solution)/shard_map/exchange/pallas_call | solution.py:130
  279.7 0.7 convert_reduce_fusion.1
  281.1 0.2 convert_reduce_fusion
  281.3 0.1 select_reduce_fusion.1
  281.4 0.2 fusion.3
  281.7 0.2 select_reduce_fusion
  281.9 0.6 compare_select_fusion.2
  282.6 3.0 copy.23
  285.6 50.8 %contract.1 = bf16[8,16,16,64,128]{4,3,2,1,0:T(8,128)(2,1)} custom-call(s32[7,48]{1,0:T(8,128)S(1)} %scatter.4.meta, bf16[32,16,128,128]{3,2,1,0:T(8,128)(2,1)} %exchange.1.x_ref, bf16[8,256,512]{2,1,0:T(8,128)(2,1)S(1)} %bitcast.24, bf16[8,512,512]{2,1,0:T(8,128)(2,1)} %all-gather.6.cloned.1.call-done.occ_ref), custom_call_target="tpu_custom_call" | custom-call | flops 17179869184 | bytes 50331648 | tf_op jit(solution)/shard_map/contract/pallas_call | solution.py:228
  (24 shorter events, 0.7 us)
Async XLA Ops:
  6.5 276.1 %all-gather.4.cloned.1.call-start = ((), (), s32[]{:S(2)}) async-start(), calls=%async_computation.1 | async-start | bytes 2359296 | tf_op jit(solution)/shard_map/all_gather | solution.py:296
  19.4 266.2 %all-gather.6.cloned.1.call-start = ((), (), s32[]{:S(2)}) async-start(), calls=%async_computation.2 | async-start | bytes 4456448 | tf_op jit(solution)/shard_map/all_gather | solution.py:297
  34.0 247.3 %copy-start = (s32[16]{0:T(128)S(1)}, s32[16]{0:T(128)}, u32[]{:S(2)}) copy-start(s32[16]{0:T(128)} %param.19) | copy-start | bytes 196
  34.0 247.3 %copy-start.1 = (s32[16]{0:T(128)S(1)}, s32[16]{0:T(128)}, u32[]{:S(2)}) copy-start(s32[16]{0:T(128)} %param.18) | copy-start | bytes 196
Sparse Core Ops, SparseCore 0:
  19.5 54.9 all-gather.3
  76.7 82.0 all-gather.5
